TPU v7x, 32 devices: a whole 2x2x4 slice. The times are simulated.
32 devices in a mesh: groups: 2 (over x), seq: 16 (over z, y, core).
Axes of the slice: x: 2, y: 2, z: 4, core: 2. Of those that a mesh axis runs over, the one named last changes fastest.
Arguments:
- queries: bfloat16 [8192, 2048], P(('groups', 'seq')), parts along dimension 0, may hold values from -9 to 9
- keys_in: bfloat16 [8192, 2048], P(('groups', 'seq')), parts along dimension 0, may hold values from -9 to 9
- values_in: bfloat16 [8192, 2048], P(('groups', 'seq')), parts along dimension 0, may hold values from -6 to 6
- cotangent: bfloat16 [8192, 2048], P(('groups', 'seq')), parts along dimension 0, may hold values from -6 to 6
- matching: int32 [32], P('groups'), parts along dimension 0, may hold values from 0 to 15, each once
- assign: int32 [32, 16], P('groups'), parts along dimension 0, may hold values from 0 to 15
Outputs:
- attended: bfloat16 [8192, 2048], P(('groups', 'seq')), parts along dimension 0
- grad_queries: bfloat16 [8192, 2048], P(('groups', 'seq')), parts along dimension 0
- grad_keys: bfloat16 [8192, 2048], P(('groups', 'seq')), parts along dimension 0
- grad_values: bfloat16 [8192, 2048], P(('groups', 'seq')), parts along dimension 0
There are 2 independent parts, one for each index of `groups`. A program takes and returns all parts, laid end to end along the dimension named above; each array names one. Nothing has to cross between parts.
Inputs may be any that keep to these rules, and one draw needn't show every extreme that they name: `matching`: each block index appears once.
All inputs are finite; a program needn't handle non-finite values.
Results may differ from a plain program's by a relative error of at most 0.019.
Values may be sent and summed in bfloat16 or wider, within the bound.
A program may use at most 128 MiB of HBM per device.

v0:
```python
import functools

import jax
import jax.numpy as jnp
from jax import lax
from jax.experimental import pallas as pl
from jax.experimental.pallas import tpu as pltpu
from jax.sharding import PartitionSpec as P

BLOCK = 256
HEADS = 16
HEAD_DIM = 128


def to_columns(panel, seq_size, slice_width):
    blocks_dev = panel.shape[0] // BLOCK
    shaped = panel.reshape(blocks_dev, BLOCK, seq_size, slice_width).transpose(2, 0, 1, 3)
    return shaped.reshape(seq_size, blocks_dev, BLOCK * slice_width)


def from_columns(moved, seq_size, slice_width):
    blocks_dev = moved.shape[1]
    shaped = moved.reshape(seq_size, blocks_dev, BLOCK, slice_width).transpose(1, 2, 0, 3)
    return shaped.reshape(blocks_dev * BLOCK, seq_size * slice_width)


def by_columns(queries, keys_in, values_in, cotangent, matching, assign):
    seq_size = lax.axis_size("seq")
    tok_dev, feature_count = queries.shape
    blocks_dev = tok_dev // BLOCK
    total_blocks = matching.shape[0]
    partner = jnp.take(matching, assign, axis=0)
    targets = jnp.arange(total_blocks, dtype=jnp.int32)
    slice_width = feature_count // seq_size
    factor = HEAD_DIM ** (-0.5)

    def column_row():
        head_here = lax.axis_index("seq") * slice_width // HEAD_DIM
        return lax.dynamic_index_in_dim(partner, head_here, 0, keepdims=False)

    shape4 = (blocks_dev, BLOCK, HEADS, HEAD_DIM)
    query_blocks = queries.reshape(shape4)
    cot_blocks = cotangent.reshape(shape4)
    row_here = column_row()
    select_here = (targets[None, :] == row_here[:, None]).astype(jnp.bfloat16)

    def pick_one(piece):
        moved = jnp.dot(
            select_here, piece.reshape(total_blocks, -1), preferred_element_type=jnp.float32
        )
        return moved.astype(jnp.bfloat16).reshape(piece.shape)

    pieces = (
        lax.all_to_all(
            to_columns(keys_in, seq_size, slice_width),
            "seq",
            split_axis=0,
            concat_axis=0,
            tiled=True,
        ),
        lax.all_to_all(
            to_columns(values_in, seq_size, slice_width),
            "seq",
            split_axis=0,
            concat_axis=0,
            tiled=True,
        ),
    )
    got_first = lax.all_to_all(pick_one(pieces[0]), "seq", split_axis=0, concat_axis=0, tiled=True)
    got_second = lax.all_to_all(pick_one(pieces[1]), "seq", split_axis=0, concat_axis=0, tiled=True)
    key_far = from_columns(got_first, seq_size, slice_width)
    value_far = from_columns(got_second, seq_size, slice_width)
    key_cat = jnp.concatenate([keys_in.reshape(shape4), key_far.reshape(shape4)], axis=1)
    value_cat = jnp.concatenate([values_in.reshape(shape4), value_far.reshape(shape4)], axis=1)
    scores = (
        jnp.einsum("bqhd,bkhd->bhqk", query_blocks, key_cat, preferred_element_type=jnp.float32)
        * factor
    )
    highest = jnp.max(scores, axis=-1, keepdims=True)
    raised = jnp.exp(scores - highest)
    weights = raised / jnp.sum(raised, axis=-1, keepdims=True)
    key_cat, value_cat, weights, weights_low = (
        key_cat,
        value_cat,
        weights,
        weights.astype(jnp.bfloat16),
    )
    out_blocks = jnp.einsum(
        "bhqk,bkhd->bqhd", weights_low, value_cat, preferred_element_type=jnp.float32
    ).astype(jnp.bfloat16)
    dprobs = jnp.einsum(
        "bqhd,bkhd->bhqk", cot_blocks, value_cat, preferred_element_type=jnp.float32
    )
    row_dot = jnp.einsum(
        "bqhd,bqhd->bhq", cot_blocks, out_blocks, preferred_element_type=jnp.float32
    )
    dscores = (weights * (dprobs - row_dot[..., None]) * factor).astype(jnp.bfloat16)
    grad_query = jnp.einsum(
        "bhqk,bkhd->bqhd", dscores, key_cat, preferred_element_type=jnp.float32
    ).astype(jnp.bfloat16)
    dkey_cat = jnp.einsum(
        "bhqk,bqhd->bkhd", dscores, query_blocks, preferred_element_type=jnp.float32
    )
    dvalue_cat = jnp.einsum(
        "bhqk,bqhd->bkhd", weights_low, cot_blocks, preferred_element_type=jnp.float32
    )
    far_keys = dkey_cat[:, BLOCK:].astype(jnp.bfloat16).reshape(tok_dev, feature_count)
    far_values = dvalue_cat[:, BLOCK:].astype(jnp.bfloat16).reshape(tok_dev, feature_count)
    row_here = column_row()
    onehot_here = (row_here[None, :] == targets[:, None]).astype(jnp.bfloat16)

    def add_columns(piece):
        summed = jnp.dot(
            onehot_here, piece.reshape(total_blocks, -1), preferred_element_type=jnp.float32
        )
        return summed.astype(jnp.bfloat16).reshape(piece.shape)

    pieces = (
        lax.all_to_all(
            to_columns(far_keys, seq_size, slice_width),
            "seq",
            split_axis=0,
            concat_axis=0,
            tiled=True,
        ),
        lax.all_to_all(
            to_columns(far_values, seq_size, slice_width),
            "seq",
            split_axis=0,
            concat_axis=0,
            tiled=True,
        ),
    )
    got_first = lax.all_to_all(
        add_columns(pieces[0]), "seq", split_axis=0, concat_axis=0, tiled=True
    )
    got_second = lax.all_to_all(
        add_columns(pieces[1]), "seq", split_axis=0, concat_axis=0, tiled=True
    )
    recv_keys = from_columns(got_first, seq_size, slice_width)
    recv_values = from_columns(got_second, seq_size, slice_width)
    grad_keys = (
        dkey_cat[:, :BLOCK].reshape(tok_dev, feature_count) + recv_keys.astype(jnp.float32)
    ).astype(jnp.bfloat16)
    grad_values = (
        dvalue_cat[:, :BLOCK].reshape(tok_dev, feature_count) + recv_values.astype(jnp.float32)
    ).astype(jnp.bfloat16)
    return (
        out_blocks.reshape(tok_dev, feature_count),
        grad_query.reshape(tok_dev, feature_count),
        grad_keys,
        grad_values,
    )


def nt(a, b):
    return lax.dot_general(a, b, (((1,), (1,)), ((), ())), preferred_element_type=jnp.float32)


def tn(a, b):
    return lax.dot_general(a, b, (((0,), (0,)), ((), ())), preferred_element_type=jnp.float32)


def nn(a, b):
    return lax.dot_general(a, b, (((1,), (0,)), ((), ())), preferred_element_type=jnp.float32)


def head_kernel(
    n,
    matching,
    assign,
    q_ref,
    k_ref,
    v_ref,
    c_ref,
    att_ref,
    gq_ref,
    gk_ref,
    gv_ref,
    q_all,
    k_all,
    v_all,
    c_all,
    att_out,
    gq_out,
    gk_out,
    gv_out,
    own_k,
    own_v,
    sum_k,
    sum_v,
    part,
    in_send,
    in_recv,
    in_local,
    out_send,
    out_recv,
    out_local,
):
    me = lax.axis_index("seq")
    factor = HEAD_DIM ** (-0.5)
    power = factor * 1.4426950408889634
    ins = ((k_ref, k_all), (v_ref, v_all), (q_ref, q_all), (c_ref, c_all))
    outs = ((att_out, att_ref), (gq_out, gq_ref), (gk_out, gk_ref), (gv_out, gv_ref))

    def columns(index):
        return pl.ds(pl.multiple_of(index * HEAD_DIM, HEAD_DIM), HEAD_DIM)

    def scatter(a, to):
        src, dst = ins[a]
        return pltpu.make_async_remote_copy(
            src_ref=src.at[:, columns(to)],
            dst_ref=dst.at[me],
            send_sem=in_send.at[a, to],
            recv_sem=in_recv.at[a, me],
            device_id={"seq": to},
            device_id_type=pl.DeviceIdType.MESH,
        )

    def arrival(a, frm):
        src, dst = ins[a]
        return pltpu.make_async_remote_copy(
            src_ref=src.at[:, columns(frm)],
            dst_ref=dst.at[frm],
            send_sem=in_send.at[a, frm],
            recv_sem=in_recv.at[a, frm],
            device_id={"seq": frm},
            device_id_type=pl.DeviceIdType.MESH,
        )

    def stay(a):
        src, dst = ins[a]
        return pltpu.make_async_copy(src.at[:, columns(me)], dst.at[me], in_local.at[a])

    def give(a, to):
        src, dst = outs[a]
        return pltpu.make_async_remote_copy(
            src_ref=src.at[to],
            dst_ref=dst.at[:, columns(me)],
            send_sem=out_send.at[a, to],
            recv_sem=out_recv.at[a, me],
            device_id={"seq": to},
            device_id_type=pl.DeviceIdType.MESH,
        )

    def returned(a, frm):
        src, dst = outs[a]
        return pltpu.make_async_remote_copy(
            src_ref=src.at[frm],
            dst_ref=dst.at[:, columns(frm)],
            send_sem=out_send.at[a, frm],
            recv_sem=out_recv.at[a, frm],
            device_id={"seq": frm},
            device_id_type=pl.DeviceIdType.MESH,
        )

    def keep(a):
        src, dst = outs[a]
        return pltpu.make_async_copy(src.at[me], dst.at[:, columns(me)], out_local.at[a])

    def over(body):
        def step(i, carry):
            body(i)
            return carry

        lax.fori_loop(1, n, step, 0)

    barrier = pltpu.get_barrier_semaphore()

    @over
    def _(i):
        to = lax.rem(me + i, n)
        pl.semaphore_signal(
            barrier, inc=1, device_id={"seq": to}, device_id_type=pl.DeviceIdType.MESH
        )

    for a in range(4):
        stay(a).start()
    pl.semaphore_wait(barrier, n - 1)

    @over
    def _(i):
        to = lax.rem(me + i, n)
        scatter(0, to).start()
        scatter(1, to).start()

    @over
    def _(i):
        to = lax.rem(me + i, n)
        scatter(2, to).start()
        scatter(3, to).start()

    def note(i, carry):
        block = lax.rem(me + n - i, n)
        part[i] = matching[assign[me, block]]
        return carry

    lax.fori_loop(0, n, note, 0)
    sum_k[...] = jnp.zeros_like(sum_k)
    sum_v[...] = jnp.zeros_like(sum_v)
    for a in range(4):
        stay(a).wait()

    @over
    def _(i):
        frm = lax.rem(me + n - i, n)
        arrival(0, frm).wait_recv()
        arrival(1, frm).wait_recv()

    def work(i):
        block = lax.rem(me + n - i, n)
        chosen = part[i]
        before = jnp.int32(n)
        for j in range(n):
            before = jnp.where((part[j] == chosen) & (j < i), jnp.int32(j), before)
        query, cot = q_all[block], c_all[block]
        key_own, key_far = k_all[block], k_all[chosen]
        value_own, value_far = v_all[block], v_all[chosen]
        s_own = nt(query, key_own) * power
        s_far = nt(query, key_far) * power
        dp_own = nt(cot, value_own)
        dp_far = nt(cot, value_far)
        highest = jnp.maximum(
            jnp.max(s_own, axis=-1, keepdims=True), jnp.max(s_far, axis=-1, keepdims=True)
        )
        e_own = jnp.exp2(s_own - highest)
        e_far = jnp.exp2(s_far - highest)
        total = jnp.sum(e_own, axis=-1, keepdims=True) + jnp.sum(e_far, axis=-1, keepdims=True)
        scale = 1.0 / total
        p_own, p_far = e_own * scale, e_far * scale
        low_own, low_far = p_own.astype(jnp.bfloat16), p_far.astype(jnp.bfloat16)
        attended = (nn(low_own, value_own) + nn(low_far, value_far)).astype(jnp.bfloat16)
        att_out[block] = attended
        row_dot = jnp.sum(
            cot.astype(jnp.float32) * attended.astype(jnp.float32), axis=-1, keepdims=True
        )
        ds_own = (p_own * (dp_own - row_dot) * factor).astype(jnp.bfloat16)
        ds_far = (p_far * (dp_far - row_dot) * factor).astype(jnp.bfloat16)
        gq_out[block] = (nn(ds_own, key_own) + nn(ds_far, key_far)).astype(jnp.bfloat16)
        own_k[block] = tn(ds_own, query)
        own_v[block] = tn(low_own, cot)
        far_k = tn(ds_far, query).astype(jnp.bfloat16).astype(jnp.float32)
        far_v = tn(low_far, cot).astype(jnp.bfloat16).astype(jnp.float32)
        sum_k[i] = sum_k[before] + far_k
        sum_v[i] = sum_v[before] + far_v

    work(0)
    keep(0).start()
    keep(1).start()

    @over
    def _(i):
        block = lax.rem(me + n - i, n)
        arrival(2, block).wait_recv()
        arrival(3, block).wait_recv()
        work(i)
        give(0, block).start()
        give(1, block).start()

    def finish(target):
        last = jnp.int32(n)
        for j in range(n):
            last = jnp.where(part[j] == target, jnp.int32(j), last)
        recv_k = sum_k[last].astype(jnp.bfloat16).astype(jnp.float32)
        recv_v = sum_v[last].astype(jnp.bfloat16).astype(jnp.float32)
        gk_out[target] = (own_k[target] + recv_k).astype(jnp.bfloat16)
        gv_out[target] = (own_v[target] + recv_v).astype(jnp.bfloat16)

    @over
    def _(i):
        target = lax.rem(me + i, n)
        finish(target)
        give(2, target).start()
        give(3, target).start()

    finish(me)
    keep(2).start()
    keep(3).start()

    @over
    def _(i):
        other = lax.rem(me + n - i, n)
        for a in range(4):
            arrival(a, other).wait_send()
            returned(a, other).wait_send()
            returned(a, other).wait_recv()

    for a in range(4):
        keep(a).wait()


def by_heads(queries, keys_in, values_in, cotangent, matching, assign):
    n = lax.axis_size("seq")
    rows, width = queries.shape
    panels = (n, rows, HEAD_DIM)
    anywhere = pl.BlockSpec(memory_space=pl.ANY)
    scalars = pl.BlockSpec(memory_space=pltpu.SMEM)
    flops = 12 * 2 * n * rows * rows * HEAD_DIM
    return pl.pallas_call(
        functools.partial(head_kernel, n),
        out_shape=[jax.ShapeDtypeStruct((rows, width), jnp.bfloat16)] * 4,
        in_specs=[scalars, scalars] + [anywhere] * 4,
        out_specs=[anywhere] * 4,
        scratch_shapes=[pltpu.VMEM(panels, jnp.bfloat16)] * 8
        + [pltpu.VMEM(panels, jnp.float32)] * 2
        + [pltpu.VMEM((n + 1, rows, HEAD_DIM), jnp.float32)] * 2
        + [
            pltpu.SMEM((n,), jnp.int32),
            pltpu.SemaphoreType.DMA((4, n)),
            pltpu.SemaphoreType.DMA((4, n)),
            pltpu.SemaphoreType.DMA((4,)),
            pltpu.SemaphoreType.DMA((4, n)),
            pltpu.SemaphoreType.DMA((4, n)),
            pltpu.SemaphoreType.DMA((4,)),
        ],
        compiler_params=pltpu.CompilerParams(
            collective_id=0, has_side_effects=True, vmem_limit_bytes=48 * 1024 * 1024
        ),
        cost_estimate=pl.CostEstimate(
            flops=flops, bytes_accessed=16 * rows * width, transcendentals=2 * n * rows * rows
        ),
    )(matching, assign, queries, keys_in, values_in, cotangent)


def per_device(queries, keys_in, values_in, cotangent, matching, assign):
    n = lax.axis_size("seq")
    if n == HEADS and queries.shape == (BLOCK, HEADS * HEAD_DIM):
        return tuple(by_heads(queries, keys_in, values_in, cotangent, matching, assign))
    return by_columns(queries, keys_in, values_in, cotangent, matching, assign)


def solution(mesh):
    in_specs = (
        P(("groups", "seq"), None),
        P(("groups", "seq"), None),
        P(("groups", "seq"), None),
        P(("groups", "seq"), None),
        P("groups"),
        P("groups", None),
    )
    out_specs = (
        P(("groups", "seq"), None),
        P(("groups", "seq"), None),
        P(("groups", "seq"), None),
        P(("groups", "seq"), None),
    )
    return jax.shard_map(
        per_device, mesh=mesh, in_specs=in_specs, out_specs=out_specs, check_vma=False
    )
```

profile of v0, /device:TPU:15, one launch (start us, length us, event | category | flops | bytes accessed | tf_op | source)
XLA Modules:
  0.0 206.9 jit_solution(4179134208326394896)
XLA Ops:
  0.6 0.0 copy-start
  0.6 1.2 copy-done
  1.9 0.0 copy-start.1
  1.9 0.7 copy-done.1
  2.6 0.0 copy-start.2
  2.6 0.7 copy-done.2
  3.2 199.8 %shard_map.93 = (bf16[256,2048]{1,0:T(8,128)(2,1)S(1)}, bf16[256,2048]{1,0:T(8,128)(2,1)S(1)}, bf16[256,2048]{1,0:T(8,128)(2,1)S(1)}, bf16[256,2048]{1,0:T(8,128)(2,1)S(1)}) custom-call(s32[16]{0:T(128)S(1)} %copy-done.2, s32[16,16]{1,0:T(8,128)S(1)} %copy-done.1, bf16[256,2048]{1,0:T(8,128)(2,1)S(1)} %copy-done, bf16[256,2048]{1,0:T(8,128)(2,1)} %k_ref.1, ...), custom_call_target="tpu_custom_call" | custom-call | flops 3221225472 | bytes 8388608 | tf_op jit(solution)/shard_map/pallas_call | solution.py:399
  203.0 1.0 copy.14
  204.0 1.0 copy.15
  205.0 1.0 copy.16
  206.0 1.0 copy.17
Async XLA Ops:
  0.6 1.2 copy-start
  1.9 0.7 copy-start.1
  2.6 0.7 copy-start.2
where the time goes:
time: 207 us
  Pallas kernels  200 us (97%)
  local copies, waits for them, and re-layouts  6.45 us (3%)
    pallas_call x1, Pallas kernels, by_heads(): pl.pallas_call(functools.partial(head_kernel, n), out_shape=[jax.ShapeDty...  200 us
    unnamed x10, local copies, waits for them, and re-layouts  6.45 us

commit v1 on v0

--- a/solution.py
+++ b/solution.py
@@ -167,8 +167,8 @@
 
 def head_kernel(
     n,
-    matching,
-    assign,
+    matching_ref,
+    assign_ref,
     q_ref,
     k_ref,
     v_ref,
@@ -189,7 +189,10 @@
     own_v,
     sum_k,
     sum_v,
+    matching,
+    assign,
     part,
+    scalar_sem,
     in_send,
     in_recv,
     in_local,
@@ -258,18 +261,40 @@
         src, dst = outs[a]
         return pltpu.make_async_copy(src.at[me], dst.at[:, columns(me)], out_local.at[a])
 
-    def over(body):
-        def step(i, carry):
-            body(i)
-            return carry
-
-        lax.fori_loop(1, n, step, 0)
+    half = n // 2
+    here = me // half
+    place = lax.rem(me, half)
+
+    def ahead(i):
+        side = lax.rem(here + i // half, 2)
+        return side * half + lax.rem(place + i, half)
+
+    def behind(i):
+        side = lax.rem(here + i // half, 2)
+        return side * half + lax.rem(place + n - i, half)
+
+    def over(start, stop):
+        def run(body):
+            def step(i, carry):
+                body(i)
+                return carry
+
+            lax.fori_loop(start, stop, step, 0)
+
+        return run
 
     barrier = pltpu.get_barrier_semaphore()
 
-    @over
+    scalars = (
+        pltpu.make_async_copy(matching_ref, matching, scalar_sem.at[0]),
+        pltpu.make_async_copy(assign_ref, assign, scalar_sem.at[1]),
+    )
+    for copy in scalars:
+        copy.start()
+
+    @over(1, n)
     def _(i):
-        to = lax.rem(me + i, n)
+        to = ahead(i)
         pl.semaphore_signal(
             barrier, inc=1, device_id={"seq": to}, device_id_type=pl.DeviceIdType.MESH
         )
@@ -278,20 +303,19 @@
         stay(a).start()
     pl.semaphore_wait(barrier, n - 1)
 
-    @over
-    def _(i):
-        to = lax.rem(me + i, n)
-        scatter(0, to).start()
-        scatter(1, to).start()
-
-    @over
-    def _(i):
-        to = lax.rem(me + i, n)
-        scatter(2, to).start()
-        scatter(3, to).start()
+    for start, stop, pair in ((half, n, (0, 1)), (half, n, (2, 3)), (1, half, (0, 1)), (1, half, (2, 3))):
+
+        @over(start, stop)
+        def _(i):
+            to = ahead(i)
+            scatter(pair[0], to).start()
+            scatter(pair[1], to).start()
+
+    for copy in scalars:
+        copy.wait()
 
     def note(i, carry):
-        block = lax.rem(me + n - i, n)
+        block = behind(i)
         part[i] = matching[assign[me, block]]
         return carry
 
@@ -301,14 +325,14 @@
     for a in range(4):
         stay(a).wait()
 
-    @over
+    @over(1, n)
     def _(i):
-        frm = lax.rem(me + n - i, n)
+        frm = behind(i)
         arrival(0, frm).wait_recv()
         arrival(1, frm).wait_recv()
 
     def work(i):
-        block = lax.rem(me + n - i, n)
+        block = behind(i)
         chosen = part[i]
         before = jnp.int32(n)
         for j in range(n):
@@ -348,9 +372,9 @@
     keep(0).start()
     keep(1).start()
 
-    @over
+    @over(1, n)
     def _(i):
-        block = lax.rem(me + n - i, n)
+        block = behind(i)
         arrival(2, block).wait_recv()
         arrival(3, block).wait_recv()
         work(i)
@@ -366,20 +390,22 @@
         gk_out[target] = (own_k[target] + recv_k).astype(jnp.bfloat16)
         gv_out[target] = (own_v[target] + recv_v).astype(jnp.bfloat16)
 
-    @over
-    def _(i):
-        target = lax.rem(me + i, n)
-        finish(target)
-        give(2, target).start()
-        give(3, target).start()
+    for start, stop in ((half, n), (1, half)):
+
+        @over(start, stop)
+        def _(i):
+            target = ahead(i)
+            finish(target)
+            give(2, target).start()
+            give(3, target).start()
 
     finish(me)
     keep(2).start()
     keep(3).start()
 
-    @over
+    @over(1, n)
     def _(i):
-        other = lax.rem(me + n - i, n)
+        other = behind(i)
         for a in range(4):
             arrival(a, other).wait_send()
             returned(a, other).wait_send()
@@ -387,6 +413,14 @@
 
     for a in range(4):
         keep(a).wait()
+
+
+def hand_over(*refs):
+    copies = [pltpu.make_async_copy(refs[a], refs[4 + a], refs[8].at[a]) for a in range(4)]
+    for copy in copies:
+        copy.start()
+    for copy in copies:
+        copy.wait()
 
 
 def by_heads(queries, keys_in, values_in, cotangent, matching, assign):
@@ -394,18 +428,20 @@
     rows, width = queries.shape
     panels = (n, rows, HEAD_DIM)
     anywhere = pl.BlockSpec(memory_space=pl.ANY)
-    scalars = pl.BlockSpec(memory_space=pltpu.SMEM)
     flops = 12 * 2 * n * rows * rows * HEAD_DIM
-    return pl.pallas_call(
+    results = pl.pallas_call(
         functools.partial(head_kernel, n),
         out_shape=[jax.ShapeDtypeStruct((rows, width), jnp.bfloat16)] * 4,
-        in_specs=[scalars, scalars] + [anywhere] * 4,
+        in_specs=[anywhere] * 6,
         out_specs=[anywhere] * 4,
         scratch_shapes=[pltpu.VMEM(panels, jnp.bfloat16)] * 8
         + [pltpu.VMEM(panels, jnp.float32)] * 2
         + [pltpu.VMEM((n + 1, rows, HEAD_DIM), jnp.float32)] * 2
         + [
+            pltpu.SMEM(matching.shape, jnp.int32),
+            pltpu.SMEM(assign.shape, jnp.int32),
             pltpu.SMEM((n,), jnp.int32),
+            pltpu.SemaphoreType.DMA((2,)),
             pltpu.SemaphoreType.DMA((4, n)),
             pltpu.SemaphoreType.DMA((4, n)),
             pltpu.SemaphoreType.DMA((4,)),
@@ -420,6 +456,14 @@
             flops=flops, bytes_accessed=16 * rows * width, transcendentals=2 * n * rows * rows
         ),
     )(matching, assign, queries, keys_in, values_in, cotangent)
+    return pl.pallas_call(
+        hand_over,
+        out_shape=[jax.ShapeDtypeStruct((rows, width), jnp.bfloat16)] * 4,
+        in_specs=[pl.BlockSpec(memory_space=pltpu.VMEM)] * 4,
+        out_specs=[anywhere] * 4,
+        scratch_shapes=[pltpu.SemaphoreType.DMA((4,))],
+        compiler_params=pltpu.CompilerParams(vmem_limit_bytes=16 * 1024 * 1024),
+    )(*results)
 
 
 def per_device(queries, keys_in, values_in, cotangent, matching, assign):

time: 207 us -> 198 us (0.957); the launches traced: 207 us -> 195 us
  Pallas kernels: 200 us -> 191 us
  local copies, waits for them, and re-layouts: 6.45 us -> 2.57 us
    pallas_call x1, Pallas kernels: 200 us -> 189 us  [by_heads(): pl.pallas_call(functools.partial(head_kernel, n), out_shape=[jax.ShapeDty...]
    unnamed x10 -> x6, local copies, waits for them, and re-layouts: 6.45 us -> 2.57 us
where the time goes in v1:
time: 198 us; the launch traced here: 195 us
  Pallas kernels  191 us (96%)
  local copies, waits for them, and re-layouts  2.57 us (1%)
    pallas_call x1, Pallas kernels, by_heads(): pl.pallas_call(functools.partial(head_kernel, n), out_shape=[jax.ShapeDty...  189 us

profile of v1, /device:TPU:15, one launch (start us, length us, event | category | flops | bytes accessed | tf_op | source)
XLA Modules:
  0.0 194.5 jit_solution(9290781942840666107)
XLA Ops:
  0.6 0.0 copy-start
  0.6 1.2 copy-done
  1.9 0.0 copy-start.1
  1.9 0.7 copy-done.1
  2.6 0.0 copy-start.2
  2.6 0.7 copy-done.2
  3.2 189.2 %shard_map.93 = (bf16[256,2048]{1,0:T(8,128)(2,1)S(1)}, bf16[256,2048]{1,0:T(8,128)(2,1)S(1)}, bf16[256,2048]{1,0:T(8,128)(2,1)S(1)}, bf16[256,2048]{1,0:T(8,128)(2,1)S(1)}) custom-call(s32[16]{0:T(128)S(1)} %copy-done.2, s32[16,16]{1,0:T(8,128)S(1)} %copy-done.1, bf16[256,2048]{1,0:T(8,128)(2,1)S(1)} %copy-done, bf16[256,2048]{1,0:T(8,128)(2,1)} %k_ref.1, ...), custom_call_target="tpu_custom_call" | custom-call | flops 3221225472 | bytes 8388608 | tf_op jit(solution)/shard_map/pallas_call | solution.py:432
  192.5 2.0 %shard_map.94 = (bf16[256,2048]{1,0:T(8,128)(2,1)}, bf16[256,2048]{1,0:T(8,128)(2,1)}, bf16[256,2048]{1,0:T(8,128)(2,1)}, bf16[256,2048]{1,0:T(8,128)(2,1)}) custom-call(bf16[256,2048]{1,0:T(8,128)(2,1)S(1)} %get-tuple-element.8.refs_0_, bf16[256,2048]{1,0:T(8,128)(2,1)S(1)} %get-tuple-element.9.refs_1_, bf16[256,2048]{1,0:T(8,128)(2,1)S(1)} %get-tuple-element.10.refs_2_, ...), custom_call_target="tpu_custom_call" | custom-call | tf_op jit(solution)/shard_map/pallas_call | solution.py:459
Async XLA Ops:
  0.6 1.2 copy-start
  1.9 0.7 copy-start.1
  2.6 0.7 copy-start.2

commit v2 on v1

--- a/solution.py
+++ b/solution.py
@@ -450,7 +450,7 @@
             pltpu.SemaphoreType.DMA((4,)),
         ],
         compiler_params=pltpu.CompilerParams(
-            collective_id=0, has_side_effects=True, vmem_limit_bytes=48 * 1024 * 1024
+            collective_id=0, has_side_effects=True, vmem_limit_bytes=52_000_000
         ),
         cost_estimate=pl.CostEstimate(
             flops=flops, bytes_accessed=16 * rows * width, transcendentals=2 * n * rows * rows

time: 198 us -> 196 us (0.990)
  no operation moved by 1% of the time
where the time goes in v2:
time: 196 us; the launch traced here: 193 us
  Pallas kernels  191 us (97%)
    pallas_call x1, Pallas kernels, by_heads(): pl.pallas_call(functools.partial(head_kernel, n), out_shape=[jax.ShapeDty...  189 us

profile of v2, /device:TPU:15, one launch (start us, length us, event | category | flops | bytes accessed | tf_op | source)
XLA Modules:
  0.0 193.3 jit_solution(12373968542743497870)
XLA Ops:
  0.6 0.0 copy-start
  0.6 0.7 copy-done
  1.3 0.0 copy-start.1
  1.3 0.7 copy-done.1
  2.0 189.2 %shard_map.93 = (bf16[256,2048]{1,0:T(8,128)(2,1)S(1)}, bf16[256,2048]{1,0:T(8,128)(2,1)S(1)}, bf16[256,2048]{1,0:T(8,128)(2,1)S(1)}, bf16[256,2048]{1,0:T(8,128)(2,1)S(1)}) custom-call(s32[16]{0:T(128)S(1)} %copy-done.1, s32[16,16]{1,0:T(8,128)S(1)} %copy-done, bf16[256,2048]{1,0:T(8,128)(2,1)} %q_ref.1, bf16[256,2048]{1,0:T(8,128)(2,1)} %k_ref.1, ...), custom_call_target="tpu_custom_call" | custom-call | flops 3221225472 | bytes 8388608 | tf_op jit(solution)/shard_map/pallas_call | solution.py:432
  191.2 2.0 %shard_map.94 = (bf16[256,2048]{1,0:T(8,128)(2,1)}, bf16[256,2048]{1,0:T(8,128)(2,1)}, bf16[256,2048]{1,0:T(8,128)(2,1)}, bf16[256,2048]{1,0:T(8,128)(2,1)}) custom-call(bf16[256,2048]{1,0:T(8,128)(2,1)S(1)} %get-tuple-element.8.refs_0_, bf16[256,2048]{1,0:T(8,128)(2,1)S(1)} %get-tuple-element.9.refs_1_, bf16[256,2048]{1,0:T(8,128)(2,1)S(1)} %get-tuple-element.10.refs_2_, ...), custom_call_target="tpu_custom_call" | custom-call | tf_op jit(solution)/shard_map/pallas_call | solution.py:459
Async XLA Ops:
  0.6 0.7 copy-start
  1.3 0.7 copy-start.1
